TPU v7x, 32 devices: a whole 2x2x4 slice. The times are simulated.
32 devices in a mesh: groups: 2 (over x), line: 16 (over z, y, core).
Axes of the slice: x: 2, y: 2, z: 4, core: 2. Of those that a mesh axis runs over, the one named last changes fastest.
Arguments:
- lodf: bfloat16 [2048, 2048], P('line'), may hold values from -0.59765625 to 0.59765625
- limits: int32 [2048], P('line'), may hold values from 50 to 150
- base_flow: float32 [4096], P(('groups', 'line')), parts along dimension 0, may hold values from -4 to 4
- first_ids: int32 [256], P(('groups', 'line')), parts along dimension 0, may hold values from 0 to 2047, as said below
- second_ids: int32 [256, 128], P(('groups', 'line')), parts along dimension 0, may hold values from 0 to 2047, as said below
- counts: int32 [256], P(('groups', 'line')), parts along dimension 0, may hold values from 1 to 128, as said below
Outputs:
- pair_penalty: float32 [256, 128], P(('groups', 'line')), parts along dimension 0
- line_pressure: float32 [4096], P(('groups', 'line')), parts along dimension 0
- lodf_grad: bfloat16 [4096, 2048], P(('groups', 'line')), parts along dimension 0
There are 2 independent parts, one for each index of `groups`. A program takes and returns all parts, laid end to end along the dimension named above; an argument that names none is the same for every part. Nothing has to cross between parts.
Inputs may be any that keep to these rules, and one draw needn't show every extreme that they name: Entry j of first_ids is a line of tile j // 8, that is between (j // 8) * 128 and (j // 8) * 128 + 127. second_ids[j, c] is a line of the same tile as first_ids[j] and differs from first_ids[j]; entries may repeat. Slots c < counts[j] of row j are live; the others are ignored.
All inputs are finite; a program needn't handle non-finite values.
Results may differ from a plain program's by a relative error of at most 0.0021.
Values may be sent and summed in bfloat16 or wider, within the bound.
No kernel may reach another device: no remote copies, remote signals or barrier semaphores. Data moves between devices by JAX's collectives and lax.ppermute only.
A program may use at most 64 MiB of HBM per device.

v0:
```python
import functools
import math

import jax
import jax.numpy as jnp
from jax import lax
from jax.experimental import pallas as pl
from jax.experimental.pallas import tpu as pltpu
from jax.sharding import PartitionSpec as P

F32 = jnp.float32
BF16 = jnp.bfloat16
CHUNK = 32


def iota(shape, dim, dtype=jnp.int32):
    return lax.broadcasted_iota(jnp.int32, shape, dim).astype(dtype)


def split3(x):
    top = x.astype(BF16).astype(F32)
    rest = x - top
    middle = rest.astype(BF16).astype(F32)
    return top, middle, rest - middle


def pack_kernel(
    first_ref, counts_ref, lodf_ref, base_ref, limits_ref, second_ref, out_ref, ids_ref
):
    width = lodf_ref.shape[0]
    firsts, cands = second_ref.shape
    peers = out_ref.shape[0]
    anchor = lax.axis_index("line") * width
    square = lodf_ref[:, pl.ds(pl.multiple_of(anchor, width), width)]
    row = iota((firsts, width), 0)
    lane = iota((firsts, width), 1)
    head = jnp.zeros((firsts, width), jnp.int32)
    lives = jnp.zeros((firsts, cands), jnp.int32)
    heads_row = jnp.zeros((1, width), F32)
    for j in range(firsts):
        local = first_ref[j] - anchor
        head = jnp.where(row == j, local, head)
        lives = jnp.where(iota((firsts, cands), 0) == j, counts_ref[j], lives)
        heads_row = jnp.where(iota((1, width), 1) == j, local.astype(F32), heads_row)
    hot = (lane == head).astype(BF16)
    first_row = jnp.dot(hot, square, preferred_element_type=F32)
    first_column = lax.dot_general(
        hot, square, (((1,), (1,)), ((), ())), preferred_element_type=F32
    )
    ids = jnp.where(iota((firsts, cands), 1) < lives, second_ref[...] - anchor, -1)
    ids_ref[...] = ids
    ones = jnp.ones((firsts, cands), BF16)
    line = iota((width, cands), 0)
    mult = jnp.zeros((firsts, width), F32)
    for j in range(firsts):
        named = (line == ids[j : j + 1]).astype(F32).astype(BF16)
        times = lax.dot_general(
            ones, named, (((1,), (1,)), ((), ())), preferred_element_type=F32
        )
        mult = jnp.where(row == j, times, mult)
    top, middle, low = split3(base_ref[...])
    limits = limits_ref[...].astype(F32)
    fill = jnp.zeros((firsts - 5, width), F32)
    block = jnp.concatenate(
        [first_row, first_column, mult, top, middle, low, heads_row, limits, fill],
        axis=0,
    )
    block = block.astype(BF16)
    for peer in range(peers):
        out_ref[peer] = block


def screen_kernel(cands, for_pairs, got_ref, lodf_ref, *refs):
    if for_pairs:
        squares_ref, kept_ref, *refs, sem = refs
        keep = pltpu.make_async_copy(got_ref, kept_ref, sem)
        keep.start()
    else:
        pressure_ref, grad_hbm, *refs, grad_ref, grad_sem, sum_ref, mult_ref, lead_ref = refs
    low_ref, high_ref, two_ref, heads_ref, at_head_ref, mix_ref, even_ref, odd_ref = refs
    tiles = got_ref.shape[0]
    width = lodf_ref.shape[0]
    firsts = got_ref.shape[1] // 4
    me = lax.axis_index("line")

    mine = got_ref[me].astype(F32)[3 * firsts :]
    base = mine[0:1] + mine[1:2] + mine[2:3]
    limit = 0.01 * mine[4:5]
    low_ref[...] = jnp.transpose(jnp.broadcast_to(-limit - base, (width, width)))
    high_ref[...] = jnp.transpose(jnp.broadcast_to(limit - base, (width, width)))

    got = got_ref[...].astype(F32)
    shape = (tiles, firsts, width)
    flat = (tiles * firsts, width)
    p = got[:, :firsts].reshape(flat)
    q = got[:, firsts : 2 * firsts].reshape(flat)
    mult = got[:, 2 * firsts : 3 * firsts].reshape(flat)
    tail = got[:, 3 * firsts :]
    flows = jnp.broadcast_to(
        tail[:, 0:1] + tail[:, 1:2] + tail[:, 2:3], shape
    ).reshape(flat)
    own = iota(shape, 2) == iota(shape, 1)
    heads = jnp.sum(
        jnp.where(own, jnp.broadcast_to(tail[:, 3:4], shape), 0.0).reshape(flat),
        axis=1,
        keepdims=True,
    )
    lane = iota(flat, 1, F32)
    first_flow = jnp.sum(jnp.where(lane == heads, flows, 0.0), axis=1, keepdims=True)
    det = 1.0 - p * q
    one = (first_flow + p * flows) / det
    two_ref[...] = (flows + q * first_flow) / det
    if not for_pairs:
        mult_ref[...] = mult
        lead_ref[...] = 2.0 * mult * one
        sum_ref[...] = jnp.zeros_like(sum_ref)
    heads_ref[...] = jnp.broadcast_to(heads, flat)

    pairs = tiles * firsts
    top = one.astype(BF16).astype(F32)
    slot = lax.rem(iota(flat, 0), firsts)
    for j in range(firsts):
        span = slice(j * width, (j + 1) * width)
        mix_ref[:pairs, span] = jnp.where(slot == j, top, 0.0).astype(BF16)
        mix_ref[pairs:, span] = jnp.where(slot == j, one - top, 0.0).astype(BF16)

    line_of = jnp.broadcast_to(heads, flat) + width * lax.div(
        iota(flat, 0), firsts
    ).astype(F32)
    line_row = jnp.transpose(line_of)[0:1]
    block = 4 * width
    at_head_ref[...] = jnp.zeros_like(at_head_ref)

    @pl.loop(0, tiles // 4, unroll=4)
    def _(step):
        start = pl.multiple_of(step * block, block)
        here = line_row - start.astype(F32)
        hot = (iota((block, pairs), 0, F32) == here).astype(F32).astype(BF16)
        at_head_ref[...] += jnp.dot(
            lodf_ref[:, pl.ds(start, block)], hot, preferred_element_type=F32
        )

    chunk = math.gcd(width, 2 * CHUNK if for_pairs else CHUNK)

    def tile_of(step):
        tile = me + step
        return jnp.where(tile >= tiles, tile - tiles, tile)

    stack = math.gcd(tiles // 2, 4 if for_pairs else 2)

    def first_terms(group, out_ref):
        parts = []
        for place in range(stack):
            tile = tile_of(stack * group + place)
            place = iota((width, pairs), 1) - tile * firsts
            part = jnp.where((place >= 0) & (place < firsts), at_head_ref[...], 0.0)
            parts.append(part.astype(BF16))
        part = jnp.concatenate(parts, axis=0)
        out_ref[...] = jnp.dot(
            jnp.concatenate([part, part], axis=1),
            mix_ref[...],
            preferred_element_type=F32,
        )

    def some_tiles(group, terms_ref, masked):
        for place in range(stack):
            one_tile(
                stack * group + place, terms_ref, place * width, masked and place == 0
            )

    def one_tile(step, terms_ref, offset, masked):
        tile = tile_of(step)
        rows = pl.ds(pl.multiple_of(tile * firsts, firsts), firsts)
        span = pl.ds(pl.multiple_of(tile * width, width), width)
        two = two_ref[rows, :]
        first = heads_ref[rows, :]
        if not for_pairs:
            twice = 2.0 * two
            mult = mult_ref[rows, :]
            lead = lead_ref[rows, :]
        squares = [jnp.zeros((8, width), F32)] * firsts
        lane = iota((chunk, width), 1, F32)
        for start in range(0, width, chunk):
            lines = slice(start, start + chunk)
            factors = lodf_ref[lines, span].astype(F32)
            low = low_ref[lines]
            high = high_ref[lines]
            if not for_pairs:
                total = sum_ref[lines]
                grad = jnp.zeros((chunk, width), F32)
            for j in range(firsts):
                pick = slice(j, j + 1)
                head = jnp.broadcast_to(first[pick], (chunk, width))
                change = (
                    terms_ref[
                        offset + start : offset + start + chunk,
                        j * width : (j + 1) * width,
                    ]
                    + factors * two[pick]
                )
                excess = change - jnp.minimum(jnp.maximum(change, low), high)
                if masked:
                    line = (iota((chunk, width), 0) + start).astype(F32)
                    excess = jnp.where((line == lane) | (line == head), 0.0, excess)
                if for_pairs:
                    squares[j] = squares[j] + jnp.sum(
                        (excess * excess).reshape(chunk // 8, 8, width), axis=0
                    )
                    continue
                total = total + excess * mult[pick]
                weighted = (excess * twice[pick]).astype(BF16).astype(F32)
                grad = grad + weighted * mult[pick]
                first_part = jnp.sum(excess * lead[pick], axis=1, keepdims=True)
                grad = grad + jnp.where(lane == head, first_part, 0.0)
            if not for_pairs:
                sum_ref[lines] = total
                grad_ref[lines, span] = (grad * (1.0 / cands)).astype(BF16)
        if for_pairs:
            squares_ref[tile] = (
                jnp.concatenate(
                    [jnp.sum(part, axis=0, keepdims=True) for part in squares], axis=0
                )
                * (1.0 / (tiles * width))
            ).astype(BF16)
        else:
            pltpu.make_async_copy(
                grad_ref.at[:, span], grad_hbm.at[:, span], grad_sem
            ).start()

    first_terms(0, even_ref)
    first_terms(1, odd_ref)
    some_tiles(0, even_ref, True)

    @pl.loop(0, tiles // (2 * stack) - 1)
    def _(turn):
        group = 2 * turn + 1
        first_terms(group + 1, even_ref)
        some_tiles(group, odd_ref, False)
        first_terms(group + 2, odd_ref)
        some_tiles(group + 1, even_ref, False)

    some_tiles(tiles // stack - 1, odd_ref, False)

    if for_pairs:
        keep.wait()
        return
    pressure_ref[...] = jnp.sum(jnp.transpose(sum_ref[...]), axis=0, keepdims=True) * (
        2.0 / (tiles * firsts * cands)
    )
    pltpu.make_async_copy(grad_ref, grad_hbm, grad_sem).wait()


def penalty_kernel(sums_ref, ids_ref, out_ref):
    sums = jnp.sum(sums_ref[...].astype(F32), axis=0)
    ids = ids_ref[...]
    found = jnp.take_along_axis(sums, jnp.maximum(ids, 0), axis=1)
    out_ref[...] = jnp.where(ids >= 0, found, 0.0)


def per_device(lodf, limits, base_flow, first_ids, second_ids, counts):
    width, lines = lodf.shape
    firsts, cands = second_ids.shape
    tiles = lax.axis_size("line")
    vmem = pl.BlockSpec(memory_space=pltpu.VMEM)
    smem = pl.BlockSpec(memory_space=pltpu.SMEM)
    hbm = pl.BlockSpec(memory_space=pl.ANY)
    base = base_flow.reshape(1, width)
    packed, ids = pl.pallas_call(
        pack_kernel,
        out_shape=(
            pltpu.VMEM((tiles, 4 * firsts, width), BF16),
            pltpu.VMEM((firsts, cands), jnp.int32),
        ),
        in_specs=[smem, smem, vmem, vmem, vmem, vmem],
        out_specs=(vmem, vmem),
        name="pack_pairs",
    )(first_ids, counts, lodf, base, limits.reshape(1, width), second_ids)
    got = lax.all_to_all(packed, "line", split_axis=0, concat_axis=0, tiled=True)
    pairs = tiles * firsts
    scratch = [
        pltpu.VMEM((width, width), F32),
        pltpu.VMEM((width, width), F32),
        pltpu.VMEM((pairs, width), F32),
        pltpu.VMEM((pairs, width), F32),
        pltpu.VMEM((width, pairs), F32),
        pltpu.VMEM((2 * pairs, firsts * width), BF16),
    ]
    terms = [
        [pltpu.VMEM((stack * width, firsts * width), F32)] * 2
        for stack in (math.gcd(tiles // 2, 4), math.gcd(tiles // 2, 2))
    ]
    params = pltpu.CompilerParams(vmem_limit_bytes=32 * 1024 * 1024)
    cost = pl.CostEstimate(
        flops=16 * width * width * pairs,
        bytes_accessed=4 * width * lines,
        transcendentals=0,
    )
    squares, kept = pl.pallas_call(
        functools.partial(screen_kernel, cands, True),
        out_shape=(
            pltpu.VMEM((tiles, firsts, width), BF16),
            jax.ShapeDtypeStruct(got.shape, BF16),
        ),
        in_specs=[vmem] * 2,
        out_specs=(vmem, hbm),
        scratch_shapes=scratch + terms[0] + [pltpu.SemaphoreType.DMA],
        compiler_params=params,
        cost_estimate=cost,
        name="screen_pairs",
    )(got, lodf)
    sums = lax.all_to_all(squares, "line", split_axis=0, concat_axis=0, tiled=True)
    pressure, grad = pl.pallas_call(
        functools.partial(screen_kernel, cands, False),
        out_shape=(
            jax.ShapeDtypeStruct((1, width), F32),
            jax.ShapeDtypeStruct((width, lines), BF16),
        ),
        in_specs=[vmem] * 2,
        out_specs=(vmem, hbm),
        scratch_shapes=scratch
        + terms[1]
        + [
            pltpu.VMEM((width, lines), BF16),
            pltpu.SemaphoreType.DMA,
            pltpu.VMEM((width, width), F32),
            pltpu.VMEM((pairs, width), F32),
            pltpu.VMEM((pairs, width), F32),
        ],
        compiler_params=params,
        cost_estimate=cost,
        name="screen_lines",
    )(kept, lodf)
    pair_penalty = pl.pallas_call(
        penalty_kernel,
        out_shape=jax.ShapeDtypeStruct((firsts, cands), F32),
        in_specs=[vmem, vmem],
        out_specs=vmem,
        compiler_params=pltpu.CompilerParams(vmem_limit_bytes=16 * 1024 * 1024),
        name="look_up",
    )(sums, ids)
    return (pair_penalty, pressure.reshape(width), grad)


def solution(mesh):
    return jax.shard_map(
        per_device,
        mesh=mesh,
        in_specs=(
            P("line", None),
            P("line"),
            P(("groups", "line")),
            P(("groups", "line")),
            P(("groups", "line"), None),
            P(("groups", "line")),
        ),
        out_specs=(P(("groups", "line"), None), P(("groups", "line")), P(("groups", "line"), None)),
        check_vma=False,
    )
```

profile of v0, /device:TPU:0, one launch (start us, length us, event | category | flops | bytes accessed | tf_op | source)
XLA Modules:
  0.0 31.8 jit_solution(16093471710900173340)
XLA Ops:
  0.6 0.0 copy-start
  0.6 1.4 %pack_pairs.1 = (bf16[16,32,128]{2,1,0:T(8,128)(2,1)S(1)}, s32[8,128]{1,0:T(8,128)S(1)}) custom-call(s32[8]{0:T(128)} %first_ref.1, s32[8]{0:T(128)} %counts_ref.1, bf16[128,2048]{1,0:T(8,128)(2,1)} %lodf_ref.5, f32[1,128]{1,0:T(1,128)} %bitcast.3, s32[1,128]{1,0:T(1,128)} %bitcast.4, s32[8,128]{1,0:T(8,128)} %second_ref.1), custom_call_target="tpu_custom_call" | custom-call | tf_op jit(solution)/shard_map/pack_pairs/pallas_call | solution.py:268
  2.1 15.1 %all_to_all.10.got_ref = bf16[16,32,128]{2,1,0:T(8,128)(2,1)S(1)} all-to-all(bf16[16,32,128]{2,1,0:T(8,128)(2,1)S(1)} %get-tuple-element.9), channel_id=1, replica_groups=mesh['groups'=2,'line'=16] {'line'}, dimensions={0} | all-to-all | bytes 262144 | tf_op jit(solution)/shard_map/all_to_all | solution.py:278
  17.2 0.0 copy-done
  17.2 3.8 %screen_pairs.1 = (bf16[16,8,128]{2,1,0:T(8,128)(2,1)}, bf16[16,32,128]{2,1,0:T(8,128)(2,1)S(1)}) custom-call(bf16[16,32,128]{2,1,0:T(8,128)(2,1)S(1)} %all_to_all.10.got_ref, bf16[128,2048]{1,0:T(8,128)(2,1)S(1)} %copy-done), custom_call_target="tpu_custom_call" | custom-call | flops 33554432 | bytes 1048576 | tf_op jit(solution)/shard_map/screen_pairs/pallas_call | solution.py:298
  20.9 3.5 %all-to-all-start.1 = ((bf16[16,8,128]{2,1,0:T(8,128)(2,1)}), bf16[16,8,128]{2,1,0:T(8,128)(2,1)S(1)}, u32[]{:S(2)}, u32[]{:S(2)}) async-start(bf16[16,8,128]{2,1,0:T(8,128)(2,1)} %get-tuple-element.10), calls=%async_computation.1 | async-start | bytes 65536 | tf_op jit(solution)/shard_map/all_to_all | solution.py:311
  24.5 6.7 %screen_lines.1 = (f32[1,128]{1,0:T(1,128)}, bf16[128,2048]{1,0:T(8,128)(2,1)}) custom-call(bf16[16,32,128]{2,1,0:T(8,128)(2,1)S(1)} %get-tuple-element.12.got_ref, bf16[128,2048]{1,0:T(8,128)(2,1)S(1)} %copy-done), custom_call_target="tpu_custom_call" | custom-call | flops 33554432 | bytes 1048576 | tf_op jit(solution)/shard_map/screen_lines/pallas_call | solution.py:312
  31.1 0.0 all-to-all-done.1.sums_ref
  31.2 0.7 %look_up.1 = f32[8,128]{1,0:T(8,128)} custom-call(bf16[16,8,128]{2,1,0:T(8,128)(2,1)S(1)} %all-to-all-done.1.sums_ref, s32[8,128]{1,0:T(8,128)S(1)} %get-tuple-element.11.ids_ref), custom_call_target="tpu_custom_call" | custom-call | tf_op jit(solution)/shard_map/look_up/pallas_call | solution.py:333
Async XLA Ops:
  0.6 16.6 %copy-start = (bf16[128,2048]{1,0:T(8,128)(2,1)S(1)}, bf16[128,2048]{1,0:T(8,128)(2,1)}, u32[]{:S(2)}) copy-start(bf16[128,2048]{1,0:T(8,128)(2,1)} %lodf_ref.5) | copy-start | bytes 1572868
  20.9 10.2 %all-to-all-start.1 = ((bf16[16,8,128]{2,1,0:T(8,128)(2,1)}), bf16[16,8,128]{2,1,0:T(8,128)(2,1)S(1)}, u32[]{:S(2)}, u32[]{:S(2)}) async-start(bf16[16,8,128]{2,1,0:T(8,128)(2,1)} %get-tuple-element.10), calls=%async_computation.1 | async-start | bytes 65536 | tf_op jit(solution)/shard_map/all_to_all | solution.py:311
where the time goes:
time: 32.1 us; the launch traced here: 31.8 us
  blocking collectives  15.1 us (47%)
  Pallas kernels  12.5 us (39%)
  starting transfers between devices  3.51 us (11%)
  between operations  0.68 us (2%)
    all_to_all x1, blocking collectives, per_device(): lax.all_to_all(packed, 'line', split_axis=0, concat_axis=0, tiled=True)  15.1 us
    pallas_call x1, Pallas kernels, per_device(): pl.pallas_call(functools.partial(screen_kernel, cands, False), out_shape=...  6.67 us
    pallas_call x1, Pallas kernels, per_device(): pl.pallas_call(functools.partial(screen_kernel, cands, True), out_shape=(...  3.75 us
    all_to_all x1, starting transfers between devices, per_device(): lax.all_to_all(squares, 'line', split_axis=0, concat_axis=0, tiled=True)  3.51 us
    pallas_call x1, Pallas kernels, per_device(): pl.pallas_call(pack_kernel, out_shape=(pltpu.VMEM((tiles, 4 * firsts, wid...  1.41 us
    pallas_call x1, Pallas kernels, per_device(): pl.pallas_call(penalty_kernel, out_shape=jax.ShapeDtypeStruct((firsts, ca...  0.68 us
  transfers between devices with their start and end apart: 1, of which 0 were waited for; matrix products, arithmetic and copies ran while one was open for 0% of the time, Pallas kernels for 21%

commit v1 on v0

--- a/solution.py
+++ b/solution.py
@@ -146,7 +146,7 @@
         tile = me + step
         return jnp.where(tile >= tiles, tile - tiles, tile)
 
-    stack = math.gcd(tiles // 2, 4 if for_pairs else 2)
+    stack = math.gcd(tiles // 2, 4)
 
     def first_terms(group, out_ref):
         parts = []
@@ -285,10 +285,7 @@
         pltpu.VMEM((width, pairs), F32),
         pltpu.VMEM((2 * pairs, firsts * width), BF16),
     ]
-    terms = [
-        [pltpu.VMEM((stack * width, firsts * width), F32)] * 2
-        for stack in (math.gcd(tiles // 2, 4), math.gcd(tiles // 2, 2))
-    ]
+    scratch += [pltpu.VMEM((math.gcd(tiles // 2, 4) * width, firsts * width), F32)] * 2
     params = pltpu.CompilerParams(vmem_limit_bytes=32 * 1024 * 1024)
     cost = pl.CostEstimate(
         flops=16 * width * width * pairs,
@@ -303,7 +300,7 @@
         ),
         in_specs=[vmem] * 2,
         out_specs=(vmem, hbm),
-        scratch_shapes=scratch + terms[0] + [pltpu.SemaphoreType.DMA],
+        scratch_shapes=scratch + [pltpu.SemaphoreType.DMA],
         compiler_params=params,
         cost_estimate=cost,
         name="screen_pairs",
@@ -318,7 +315,6 @@
         in_specs=[vmem] * 2,
         out_specs=(vmem, hbm),
         scratch_shapes=scratch
-        + terms[1]
         + [
             pltpu.VMEM((width, lines), BF16),
             pltpu.SemaphoreType.DMA,

time: 32.1 us -> 32.3 us (level)
  no operation moved by 1% of the time
where the time goes in v1:
time: 32.3 us; the launch traced here: 32 us
  blocking collectives  15.1 us (47%)
  Pallas kernels  12.7 us (39%)
  starting transfers between devices  3.51 us (11%)
  between operations  0.68 us (2%)
    all_to_all x1, blocking collectives, per_device(): lax.all_to_all(packed, 'line', split_axis=0, concat_axis=0, tiled=True)  15.1 us
    pallas_call x1, Pallas kernels, per_device(): pl.pallas_call(functools.partial(screen_kernel, cands, False), out_shape=...  6.88 us
    pallas_call x1, Pallas kernels, per_device(): pl.pallas_call(functools.partial(screen_kernel, cands, True), out_shape=(...  3.75 us
    all_to_all x1, starting transfers between devices, per_device(): lax.all_to_all(squares, 'line', split_axis=0, concat_axis=0, tiled=True)  3.51 us
    pallas_call x1, Pallas kernels, per_device(): pl.pallas_call(pack_kernel, out_shape=(pltpu.VMEM((tiles, 4 * firsts, wid...  1.41 us
    pallas_call x1, Pallas kernels, per_device(): pl.pallas_call(penalty_kernel, out_shape=jax.ShapeDtypeStruct((firsts, ca...  0.68 us
  transfers between devices with their start and end apart: 1, of which 0 were waited for; matrix products, arithmetic and copies ran while one was open for 0% of the time, Pallas kernels for 21%

profile of v1, /device:TPU:0, one launch (start us, length us, event | category | flops | bytes accessed | tf_op | source)
XLA Modules:
  0.0 32.0 jit_solution(3252733442449153179)
XLA Ops:
  0.6 0.0 copy-start
  0.6 1.4 %pack_pairs.1 = (bf16[16,32,128]{2,1,0:T(8,128)(2,1)S(1)}, s32[8,128]{1,0:T(8,128)S(1)}) custom-call(s32[8]{0:T(128)} %first_ref.1, s32[8]{0:T(128)} %counts_ref.1, bf16[128,2048]{1,0:T(8,128)(2,1)} %lodf_ref.5, f32[1,128]{1,0:T(1,128)} %bitcast.3, s32[1,128]{1,0:T(1,128)} %bitcast.4, s32[8,128]{1,0:T(8,128)} %second_ref.1), custom_call_target="tpu_custom_call" | custom-call | tf_op jit(solution)/shard_map/pack_pairs/pallas_call | solution.py:268
  2.1 15.1 %all_to_all.10.got_ref = bf16[16,32,128]{2,1,0:T(8,128)(2,1)S(1)} all-to-all(bf16[16,32,128]{2,1,0:T(8,128)(2,1)S(1)} %get-tuple-element.9), channel_id=1, replica_groups=mesh['groups'=2,'line'=16] {'line'}, dimensions={0} | all-to-all | bytes 262144 | tf_op jit(solution)/shard_map/all_to_all | solution.py:278
  17.2 0.0 copy-done
  17.2 3.8 %screen_pairs.1 = (bf16[16,8,128]{2,1,0:T(8,128)(2,1)}, bf16[16,32,128]{2,1,0:T(8,128)(2,1)S(1)}) custom-call(bf16[16,32,128]{2,1,0:T(8,128)(2,1)S(1)} %all_to_all.10.got_ref, bf16[128,2048]{1,0:T(8,128)(2,1)S(1)} %copy-done), custom_call_target="tpu_custom_call" | custom-call | flops 33554432 | bytes 1048576 | tf_op jit(solution)/shard_map/screen_pairs/pallas_call | solution.py:295
  20.9 3.5 %all-to-all-start.1 = ((bf16[16,8,128]{2,1,0:T(8,128)(2,1)}), bf16[16,8,128]{2,1,0:T(8,128)(2,1)S(1)}, u32[]{:S(2)}, u32[]{:S(2)}) async-start(bf16[16,8,128]{2,1,0:T(8,128)(2,1)} %get-tuple-element.10), calls=%async_computation.1 | async-start | bytes 65536 | tf_op jit(solution)/shard_map/all_to_all | solution.py:308
  24.5 6.9 %screen_lines.1 = (f32[1,128]{1,0:T(1,128)}, bf16[128,2048]{1,0:T(8,128)(2,1)}) custom-call(bf16[16,32,128]{2,1,0:T(8,128)(2,1)S(1)} %get-tuple-element.12.got_ref, bf16[128,2048]{1,0:T(8,128)(2,1)S(1)} %copy-done), custom_call_target="tpu_custom_call" | custom-call | flops 33554432 | bytes 1048576 | tf_op jit(solution)/shard_map/screen_lines/pallas_call | solution.py:309
  31.3 0.0 all-to-all-done.1.sums_ref
  31.4 0.7 %look_up.1 = f32[8,128]{1,0:T(8,128)} custom-call(bf16[16,8,128]{2,1,0:T(8,128)(2,1)S(1)} %all-to-all-done.1.sums_ref, s32[8,128]{1,0:T(8,128)S(1)} %get-tuple-element.11.ids_ref), custom_call_target="tpu_custom_call" | custom-call | tf_op jit(solution)/shard_map/look_up/pallas_call | solution.py:329
Async XLA Ops:
  0.6 16.6 %copy-start = (bf16[128,2048]{1,0:T(8,128)(2,1)S(1)}, bf16[128,2048]{1,0:T(8,128)(2,1)}, u32[]{:S(2)}) copy-start(bf16[128,2048]{1,0:T(8,128)(2,1)} %lodf_ref.5) | copy-start | bytes 1572868
  20.9 10.4 %all-to-all-start.1 = ((bf16[16,8,128]{2,1,0:T(8,128)(2,1)}), bf16[16,8,128]{2,1,0:T(8,128)(2,1)S(1)}, u32[]{:S(2)}, u32[]{:S(2)}) async-start(bf16[16,8,128]{2,1,0:T(8,128)(2,1)} %get-tuple-element.10), calls=%async_computation.1 | async-start | bytes 65536 | tf_op jit(solution)/shard_map/all_to_all | solution.py:308
